TPU v7x, 512 devices: a whole 4x8x8 slice. The times are simulated.
512 devices in a mesh: segment: 4 (over x), blk: 128 (over z, y, core).
Axes of the slice: x: 4, y: 8, z: 8, core: 2. Of those that a mesh axis runs over, the one named last changes fastest.
Arguments:
- inputs: bfloat16 [32, 65536], P('segment', 'blk'), may hold values from 0 to 24
- weights: bfloat16 [8, 512, 2048, 128], P('segment', 'blk'), may hold values from -0.1875 to 0.1875
- biases: float32 [8, 65536], P('segment', 'blk'), may hold values from -32 to 32
- sources: int32 [8, 512, 16], P('segment', 'blk'), may hold values from 0 to 511, as said below
- send_slot: int32 [8, 128, 128, 1], P('segment', 'blk'), may hold values from 0 to 4, as said below
Outputs:
- activations_out: bfloat16 [32, 65536], P('segment', 'blk')
Inputs may be any that keep to these rules, and one draw needn't show every extreme that they name: `sources`: the 16 ids of one output block are distinct and no two of them share both owner g // 4 and residue g % 1; every id g of an output block owned by device d equals p * 4 + send_slot[l, p, d, g % 1] with p = g // 4. send_slot[l, p, d, s] is 4 where device d reads no block of device p with residue s in layer l, else a local block index whose residue modulo 1 is s.
All inputs are finite; a program needn't handle non-finite values.
Results may differ from a plain program's by a relative error of at most 0.011.
Values may be sent and summed in bfloat16 or wider, within the bound.
A program may use at most 64 MiB of HBM per device.

v0:
```python
import jax
import jax.numpy as jnp
from jax import lax
from jax.experimental import pallas as pl
from jax.experimental.pallas import tpu as pltpu
from jax.sharding import PartitionSpec as P

MESH = pl.DeviceIdType.MESH
CEILING = 32.0
SIDE = 8
READERS = 2 * SIDE * SIDE
SECTIONS = 4
BLOCKS = 4
FAN = 16
ROWS = 8
WIDTH = 128
NAMES = ("one", "two", "three", "four")


def kernel(
    inputs_hbm, weights_hbm, biases_hbm, sources_hbm, slots_hbm, out_ref,
    held, first_0, first_1, first_2, first_3, second_0, second_1, second_2, second_3,
    first_out, second_out, start_out, inputs_ref, tiles, biases_ref, sources_ref,
    slots_ref, slot_rows, start_rows, next_rows, start_slots, next_slots, result, landed,
    first_recv, second_recv, first_send, second_send, start_send,
    load_sem, row_send, start_row_recv, next_row_recv, table_sem, land_send, land_recv, hello,
):
    first_in = (first_0, first_1, first_2, first_3)
    second_in = (second_0, second_1, second_2, second_3)
    section = lax.axis_index("segment")
    me = lax.axis_index("blk")
    z, y, core = me // (2 * SIDE), (me // 2) % SIDE, me % 2
    last = SECTIONS - 1
    middle = SIDE // 2

    loads = [
        pltpu.make_async_copy(source, target, load_sem.at[i])
        for i, (source, target) in enumerate((
            (inputs_hbm, inputs_ref),
            (slots_hbm, slots_ref),
            (slots_hbm, slot_rows),
            (sources_hbm, sources_ref),
            (biases_hbm, biases_ref),
            (weights_hbm, tiles),
        ))
    ]
    for load in loads:
        load.start()

    def each_chip(act):
        def chip(dz, dy):
            row = (z + dz + SIDE) % SIDE * SIDE + (y + dy + SIDE) % SIDE
            act(2 * row)
            act(2 * row + 1)

        def some(total, carry):
            total = SIDE - total

            def pair(far_z, inner):
                far_y = total - far_z
                turn_z = jnp.logical_and(far_z > 0, far_z < middle)
                turn_y = jnp.logical_and(far_y > 0, far_y < middle)
                chip(far_z, far_y)

                @pl.when(jnp.logical_and(turn_z, turn_y))
                def _():
                    chip(-far_z, -far_y)

                @pl.when(turn_z)
                def _():
                    chip(-far_z, far_y)

                @pl.when(turn_y)
                def _():
                    chip(far_z, -far_y)

                return inner

            return lax.fori_loop(jnp.maximum(total - middle, 0), jnp.minimum(total, middle) + 1, pair, carry)

        lax.fori_loop(0, SIDE, some, 0)

    barrier = pltpu.get_barrier_semaphore()

    def greet(reader):
        pl.semaphore_signal(barrier, inc=1, device_id=(section, reader), device_id_type=MESH)

    sibling = me + 1 - 2 * core
    with jax.named_scope("enter"):

        @pl.when(section == 0)
        def _():
            for other in range(1, SECTIONS):
                pl.semaphore_signal(barrier, inc=1, device_id=(other, me), device_id_type=MESH)

        @pl.when(jnp.logical_and(section > 0, section < last))
        def _():
            pl.semaphore_signal(barrier, inc=1, device_id=(section + 1, me), device_id_type=MESH)

        each_chip(greet)
        greet(sibling)
        for load in loads[:3]:
            load.wait()
        for block in range(BLOCKS):
            held[block] = inputs_ref[:, block * WIDTH : (block + 1) * WIDTH]
        pl.semaphore_wait(barrier, READERS - 1 + jnp.minimum(section, 2))

    def send_rows(target, arriving, send_sem, recv_sem):
        pltpu.make_async_remote_copy(
            src_ref=slot_rows,
            dst_ref=arriving,
            send_sem=send_sem,
            recv_sem=recv_sem,
            device_id=(target, me),
            device_id_type=MESH,
        ).start()

    def full(ref, sem):
        pltpu.make_async_copy(ref, ref, sem).wait()

    def exchange(slot_of, outgoing, target, arriving, send_sem, recv_sem, own):
        def put(reader):
            outgoing[reader] = held[jnp.minimum(slot_of(reader), BLOCKS - 1)]

        def post(reader):
            put(reader)
            pltpu.make_async_remote_copy(
                src_ref=outgoing.at[reader],
                dst_ref=arriving.at[me],
                send_sem=send_sem,
                recv_sem=recv_sem,
                device_id=(target, reader),
                device_id_type=MESH,
            ).start()

        each_chip(post)
        post(sibling)
        if own:
            arriving[me] = held[jnp.minimum(slot_of(me), BLOCKS - 1)]
        else:
            post(me)

    def arrived(ref, count, sem):
        part = ref.at[pl.ds(0, count)]
        pltpu.make_async_copy(part, part, sem).wait()

    def layer(index, arriving):
        for block in range(BLOCKS):
            parts = [arriving[sources_ref[index, block, k] // BLOCKS] for k in range(FAN)]
            summed = jnp.dot(
                jnp.concatenate(parts, axis=1),
                tiles[index, block],
                preferred_element_type=jnp.float32,
            )
            shifted = summed + biases_ref[index : index + 1, block * WIDTH : (block + 1) * WIDTH]
            held[block] = jnp.clip(shifted, 0.0, CEILING).astype(jnp.bfloat16)

    def to_table(rows, table):
        copy = pltpu.make_async_copy(rows, table, table_sem)
        copy.start()
        copy.wait()

    with jax.named_scope("start"):

        @pl.when(section == 0)
        def _():
            exchange(
                lambda reader: slots_ref[0, reader],
                start_out, 0, first_0, start_send, first_recv.at[0], True,
            )
            full(next_rows, next_row_recv)
            send_rows(1, start_rows, row_send.at[0], start_row_recv)
            pl.semaphore_wait(hello.at[0], 1)
            send_rows(2, start_rows, row_send.at[1], start_row_recv)

        @pl.when(section > 0)
        def _():
            send_rows(section - 1, next_rows, row_send.at[0], next_row_recv)

        for batch in range(1, SECTIONS):

            @pl.when(section == batch)
            def _():
                if batch > 1:
                    pl.semaphore_signal(hello.at[batch - 2], inc=1, device_id=(0, me), device_id_type=MESH)
                full(start_rows, start_row_recv)
                to_table(start_rows, start_slots)
                exchange(
                    lambda reader: start_slots[0, reader],
                    start_out, 0, first_in[batch], start_send, first_recv.at[batch], False,
                )

        for load in loads[3:]:
            load.wait()

    def first(batch):
        name = NAMES[batch]
        with jax.named_scope("wait a " + name):
            if batch == 0:

                @pl.when(section == 0)
                def _():
                    arrived(first_0, READERS - 1, first_recv.at[0])

                @pl.when(section > 0)
                def _():
                    full(first_0, first_recv.at[0])

            else:
                full(first_in[batch], first_recv.at[batch])
        with jax.named_scope("layer a " + name):
            layer(0, first_in[batch])
        with jax.named_scope("send a " + name):
            exchange(
                lambda reader: slots_ref[1, reader], second_out.at[batch], section,
                second_in[batch], second_send.at[batch], second_recv.at[batch], True,
            )

    def second(batch):
        name = NAMES[batch]
        with jax.named_scope("wait b " + name):
            arrived(second_in[batch], READERS - 1, second_recv.at[batch])
        with jax.named_scope("layer b " + name):
            layer(1, second_in[batch])
        with jax.named_scope("send b " + name):

            @pl.when(section < last)
            def _():
                exchange(
                    lambda reader: next_slots[0, reader], first_out.at[batch], section + 1,
                    first_in[batch], first_send.at[batch], first_recv.at[batch], False,
                )

            @pl.when(section == last)
            def _():
                for block in range(BLOCKS):
                    scaled = held[block].astype(jnp.float32) * (1.0 / CEILING)
                    result[batch, :, block * WIDTH : (block + 1) * WIDTH] = scaled.astype(jnp.bfloat16)
                if batch < last:
                    pltpu.make_async_remote_copy(
                        src_ref=result.at[batch],
                        dst_ref=landed,
                        send_sem=land_send,
                        recv_sem=land_recv,
                        device_id=(batch, me),
                        device_id_type=MESH,
                    ).start()

    for step in range(SECTIONS + 1):
        if step < SECTIONS:
            first(step)
        if step == 0:

            @pl.when(section == 0)
            def _():
                pl.semaphore_wait(hello.at[1], 1)
                send_rows(3, start_rows, row_send.at[2], start_row_recv)
                to_table(next_rows, next_slots)

            @pl.when(jnp.logical_and(section > 0, section < last))
            def _():
                full(next_rows, next_row_recv)
                to_table(next_rows, next_slots)

        if step > 0:
            second(step - 1)

    with jax.named_scope("leave"):
        full(slot_rows, row_send.at[0])

        @pl.when(section == 0)
        def _():
            full(slot_rows, row_send.at[1])
            full(slot_rows, row_send.at[2])
            arrived(start_out, READERS - 1, start_send)

        @pl.when(section > 0)
        def _():
            full(start_out, start_send)

        for batch in range(SECTIONS):
            arrived(second_out.at[batch], READERS - 1, second_send.at[batch])

        @pl.when(section < last)
        def _():
            for batch in range(SECTIONS):
                full(first_out.at[batch], first_send.at[batch])
            full(landed, land_recv)
            out_ref[...] = landed[...]

        @pl.when(section == last)
        def _():
            full(result.at[pl.ds(0, SECTIONS - 1)], land_send)
            out_ref[...] = result[last]


def per_device(inputs, weights, biases, sources, send_slot):
    slots = send_slot.reshape(2, READERS)
    bf16 = jnp.bfloat16
    pool = (READERS, ROWS, WIDTH)
    dma = pltpu.SemaphoreType.DMA
    return pl.pallas_call(
        kernel,
        out_shape=jax.ShapeDtypeStruct((ROWS, BLOCKS * WIDTH), bf16),
        in_specs=[pl.BlockSpec(memory_space=pltpu.HBM)] * 5,
        out_specs=pl.BlockSpec(memory_space=pltpu.VMEM),
        scratch_shapes=[
            pltpu.VMEM((BLOCKS, ROWS, WIDTH), bf16),
            *[pltpu.VMEM(pool, bf16)] * (2 * SECTIONS),
            pltpu.VMEM((SECTIONS, *pool), bf16),
            pltpu.VMEM((SECTIONS, *pool), bf16),
            pltpu.VMEM(pool, bf16),
            pltpu.VMEM(inputs.shape, bf16),
            pltpu.VMEM(weights.shape, bf16),
            pltpu.VMEM(biases.shape, jnp.float32),
            pltpu.SMEM(sources.shape, jnp.int32),
            pltpu.SMEM(slots.shape, jnp.int32),
            pltpu.VMEM(slots.shape, jnp.int32),
            pltpu.VMEM(slots.shape, jnp.int32),
            pltpu.VMEM(slots.shape, jnp.int32),
            pltpu.SMEM(slots.shape, jnp.int32),
            pltpu.SMEM(slots.shape, jnp.int32),
            pltpu.VMEM((SECTIONS, ROWS, BLOCKS * WIDTH), bf16),
            pltpu.VMEM((ROWS, BLOCKS * WIDTH), bf16),
            dma((SECTIONS,)),
            dma((SECTIONS,)),
            dma((SECTIONS,)),
            dma((SECTIONS,)),
            dma(()),
            dma((6,)),
            dma((SECTIONS - 1,)),
            dma(()),
            dma(()),
            dma(()),
            dma(()),
            dma(()),
            pltpu.SemaphoreType.REGULAR((2,)),
        ],
        compiler_params=pltpu.CompilerParams(
            collective_id=0, has_side_effects=True, vmem_limit_bytes=60 * 2**20
        ),
        cost_estimate=pl.CostEstimate(flops=2**28, bytes_accessed=2**23, transcendentals=0),
    )(inputs, weights, biases, sources, slots)


def solution(mesh):
    placed = (
        P("segment", "blk"),
        P("segment", "blk", None, None),
        P("segment", "blk"),
        P("segment", "blk", None),
        P("segment", "blk", None, None),
    )
    return jax.shard_map(
        per_device, mesh=mesh, in_specs=placed, out_specs=P("segment", "blk"), check_vma=False
    )
```

profile of v0, /device:TPU:7, one launch (start us, length us, event | category | flops | bytes accessed | tf_op | source)
XLA Modules:
  0.0 150.9 jit_solution(13791468341750743227)
XLA Ops:
  0.0 149.5 %shard_map.55 = bf16[8,512]{1,0:T(8,128)(2,1)} custom-call(bf16[8,512]{1,0:T(8,128)(2,1)} %inputs_hbm.1, bf16[2,4,2048,128]{3,2,1,0:T(8,128)(2,1)} %weights_hbm.1, f32[2,512]{1,0:T(2,128)} %biases_hbm.1, s32[2,4,16]{2,1,0:T(4,128)} %sources_hbm.1, s32[2,128]{1,0:T(2,128)} %bitcast.1), custom_call_target="tpu_custom_call" | custom-call | flops 268435456 | bytes 8388608 | tf_op jit(solution)/shard_map/pallas_call | solution.py:302
  149.6 1.3 copy.7
where the time goes:
time: 151 us
  Pallas kernels  150 us (99%)
    pallas_call x1, Pallas kernels, per_device(): pl.pallas_call(kernel, out_shape=jax.ShapeDtypeStruct((ROWS, BLOCKS * WID...  150 us

commit v1 on v0

v1 whole, which is shorter than its diff:
```python
import jax
import jax.numpy as jnp
from jax import lax
from jax.experimental import pallas as pl
from jax.experimental.pallas import tpu as pltpu
from jax.sharding import PartitionSpec as P

MESH = pl.DeviceIdType.MESH
CEILING = 32.0
SIDE = 8
READERS = 2 * SIDE * SIDE
SECTIONS = 4
BLOCKS = 4
FAN = 16
ROWS = 8
WIDTH = 128
FAR = (4, 3, 5, 2, 6, 1, 7, 0)
RELAYED = 2 * SIDE - 1


def kernel(
    inputs_hbm, weights_hbm, biases_hbm, sources_hbm, slots_hbm, out_ref,
    held, first_0, first_1, first_2, first_3, second_0, second_1, second_2, second_3,
    first_out, second_out, start_out, inputs_ref, tiles, biases_ref, sources_ref,
    slots_ref, slot_rows, start_rows, next_rows, start_slots, next_slots, result, landed,
    first_recv, second_recv, first_send, second_send, start_send,
    relay_in, relay_recv, bundle_send, relay_send,
    load_sem, row_send, start_row_recv, next_row_recv, table_sem, land_send, land_recv, hello,
):
    first_in = (first_0, first_1, first_2, first_3)
    second_in = (second_0, second_1, second_2, second_3)
    section = lax.axis_index("segment")
    me = lax.axis_index("blk")
    z, y, core = me // (2 * SIDE), (me // 2) % SIDE, me % 2
    last = SECTIONS - 1
    middle = SIDE // 2
    other = 1 - core
    across_z, across_y = (z + middle) % SIDE, (y + middle) % SIDE

    loads = [
        pltpu.make_async_copy(source, target, load_sem.at[i])
        for i, (source, target) in enumerate((
            (inputs_hbm, inputs_ref),
            (slots_hbm, slots_ref),
            (slots_hbm, slot_rows),
            (sources_hbm, sources_ref),
            (biases_hbm, biases_ref),
            (weights_hbm, tiles),
        ))
    ]
    for load in loads:
        load.start()

    def place(at_z, at_y, at_core):
        return (at_z * SIDE + at_y) * 2 + at_core

    def each_chip(act):
        def some(step, carry):
            total = SIDE - step

            def pair(far_z, inner):
                far_y = total - far_z
                turn_z = jnp.logical_and(far_z > 0, far_z < middle)
                turn_y = jnp.logical_and(far_y > 0, far_y < middle)
                near = jnp.logical_and(far_z < middle, far_y < middle)

                def chip(dz, dy):
                    at_z, at_y = (z + dz + SIDE) % SIDE, (y + dy + SIDE) % SIDE
                    act(at_z, at_y, core)

                    @pl.when(near)
                    def _():
                        act(at_z, at_y, other)

                chip(far_z, far_y)

                @pl.when(jnp.logical_and(turn_z, turn_y))
                def _():
                    chip(-far_z, -far_y)

                @pl.when(turn_z)
                def _():
                    chip(-far_z, far_y)

                @pl.when(turn_y)
                def _():
                    chip(far_z, -far_y)

                return inner

            return lax.fori_loop(jnp.maximum(total - middle, 0), jnp.minimum(total, middle) + 1, pair, carry)

        lax.fori_loop(0, SIDE, some, 0)

    barrier = pltpu.get_barrier_semaphore()

    def greet(step, carry):
        reader = (me + step) % READERS
        pl.semaphore_signal(barrier, inc=1, device_id=(section, reader), device_id_type=MESH)
        return carry


    @pl.when(section == 0)
    def _():
        for later in range(1, SECTIONS):
            pl.semaphore_signal(barrier, inc=1, device_id=(later, me), device_id_type=MESH)

    @pl.when(jnp.logical_and(section > 0, section < last))
    def _():
        pl.semaphore_signal(barrier, inc=1, device_id=(section + 1, me), device_id_type=MESH)

    lax.fori_loop(1, READERS, greet, 0)
    for load in loads[:3]:
        load.wait()
    for block in range(BLOCKS):
        held[block] = inputs_ref[:, block * WIDTH : (block + 1) * WIDTH]
    pl.semaphore_wait(barrier, READERS - 1 + jnp.minimum(section, 2))

    def send_rows(target, arriving, send_sem, recv_sem):
        pltpu.make_async_remote_copy(
            src_ref=slot_rows,
            dst_ref=arriving,
            send_sem=send_sem,
            recv_sem=recv_sem,
            device_id=(target, me),
            device_id_type=MESH,
        ).start()

    def full(ref, sem):
        pltpu.make_async_copy(ref, ref, sem).wait()

    def exchange(index, slot_of, outgoing, target, arriving, send_sem, recv_sem, own):
        def pick(at_z, at_y, at_core):
            return held[jnp.minimum(slot_of(place(at_z, at_y, at_core)), BLOCKS - 1)]

        def put(at_z, at_y, at_core):
            outgoing[at_z, at_y, at_core] = pick(at_z, at_y, at_core)

        def post(at_z, at_y, at_core):
            put(at_z, at_y, at_core)
            pltpu.make_async_remote_copy(
                src_ref=outgoing.at[at_z, at_y, at_core],
                dst_ref=arriving.at[me],
                send_sem=send_sem,
                recv_sem=recv_sem,
                device_id=(target, place(at_z, at_y, at_core)),
                device_id_type=MESH,
            ).start()

        for step in range(SIDE):
            put(step, across_y, other)
        for step in range(SIDE):
            put(across_z, step, other)
        bundles = (
            (outgoing.at[:, across_y, other], place(z, (y + SIDE - 1) % SIDE, core)),
            (outgoing.at[across_z, :, other], place((z + SIDE - 1) % SIDE, y, core)),
        )
        for side, (bundle, relay_at) in enumerate(bundles):
            pltpu.make_async_remote_copy(
                src_ref=bundle,
                dst_ref=relay_in.at[index, side],
                send_sem=bundle_send.at[index],
                recv_sem=relay_recv.at[index, side],
                device_id=(section, relay_at),
                device_id_type=MESH,
            ).start()
        each_chip(post)
        post(z, y, other)
        if own:
            arriving[me] = pick(z, y, core)
        else:
            post(z, y, core)

        def forward(side, step, origin, at_z, at_y):
            pltpu.make_async_remote_copy(
                src_ref=relay_in.at[index, side, step],
                dst_ref=arriving.at[origin],
                send_sem=relay_send.at[index],
                recv_sem=recv_sem,
                device_id=(target, place(at_z, at_y, other)),
                device_id_type=MESH,
            ).start()

        full(relay_in.at[index, 0], relay_recv.at[index, 0])
        for far in FAR:
            step = (z + far) % SIDE
            forward(0, step, place(z, (y + 1) % SIDE, core), step, (y + 1 + middle) % SIDE)
        full(relay_in.at[index, 1], relay_recv.at[index, 1])
        for far in FAR[1:]:
            step = (y + far) % SIDE
            forward(1, step, place((z + 1) % SIDE, y, core), (z + 1 + middle) % SIDE, step)

    def arrived(ref, count, sem):
        part = ref.at[pl.ds(0, count)]
        pltpu.make_async_copy(part, part, sem).wait()

    def layer(index, arriving):
        for block in range(BLOCKS):
            parts = [arriving[sources_ref[index, block, k] // BLOCKS] for k in range(FAN)]
            summed = jnp.dot(
                jnp.concatenate(parts, axis=1),
                tiles[index, block],
                preferred_element_type=jnp.float32,
            )
            shifted = summed + biases_ref[index : index + 1, block * WIDTH : (block + 1) * WIDTH]
            held[block] = jnp.clip(shifted, 0.0, CEILING).astype(jnp.bfloat16)

    def to_table(rows, table):
        copy = pltpu.make_async_copy(rows, table, table_sem)
        copy.start()
        copy.wait()


    @pl.when(section == 0)
    def _():
        exchange(
            0, lambda reader: slots_ref[0, reader],
            start_out, 0, first_0, start_send, first_recv.at[0], True,
        )
        full(next_rows, next_row_recv)
        send_rows(1, start_rows, row_send.at[0], start_row_recv)
        pl.semaphore_wait(hello.at[0], 1)
        send_rows(2, start_rows, row_send.at[1], start_row_recv)

    @pl.when(section > 0)
    def _():
        send_rows(section - 1, next_rows, row_send.at[0], next_row_recv)

    for batch in range(1, SECTIONS):

        @pl.when(section == batch)
        def _():
            if batch > 1:
                pl.semaphore_signal(hello.at[batch - 2], inc=1, device_id=(0, me), device_id_type=MESH)
            full(start_rows, start_row_recv)
            to_table(start_rows, start_slots)
            exchange(
                0, lambda reader: start_slots[0, reader],
                start_out, 0, first_in[batch], start_send, first_recv.at[batch], False,
            )

    for load in loads[3:]:
        load.wait()

    def first(batch):
        if batch == 0:

            @pl.when(section == 0)
            def _():
                arrived(first_0, READERS - 1, first_recv.at[0])

            @pl.when(section > 0)
            def _():
                full(first_0, first_recv.at[0])

        else:
            full(first_in[batch], first_recv.at[batch])
        layer(0, first_in[batch])
        exchange(
            1 + batch, lambda reader: slots_ref[1, reader], second_out.at[batch], section,
            second_in[batch], second_send.at[batch], second_recv.at[batch], True,
        )

    def second(batch):
        arrived(second_in[batch], READERS - 1, second_recv.at[batch])
        layer(1, second_in[batch])

        @pl.when(section < last)
        def _():
            exchange(
                1 + SECTIONS + batch, lambda reader: next_slots[0, reader], first_out.at[batch], section + 1,
                first_in[batch], first_send.at[batch], first_recv.at[batch], False,
            )

        @pl.when(section == last)
        def _():
            for block in range(BLOCKS):
                scaled = held[block].astype(jnp.float32) * (1.0 / CEILING)
                result[batch, :, block * WIDTH : (block + 1) * WIDTH] = scaled.astype(jnp.bfloat16)
            if batch < last:
                pltpu.make_async_remote_copy(
                    src_ref=result.at[batch],
                    dst_ref=landed,
                    send_sem=land_send,
                    recv_sem=land_recv,
                    device_id=(batch, me),
                    device_id_type=MESH,
                ).start()

    first(0)

    @pl.when(section == 0)
    def _():
        pl.semaphore_wait(hello.at[1], 1)
        send_rows(3, start_rows, row_send.at[2], start_row_recv)
        to_table(next_rows, next_slots)

    @pl.when(jnp.logical_and(section > 0, section < last))
    def _():
        full(next_rows, next_row_recv)
        to_table(next_rows, next_slots)

    first(1)
    second(0)
    second(1)
    first(2)
    first(3)
    second(2)
    second(3)

    full(slot_rows, row_send.at[0])

    def gone(index, count, sem):
        arrived(first_0, count, sem)
        full(relay_in.at[index], bundle_send.at[index])
        arrived(first_0, RELAYED, relay_send.at[index])

    direct = READERS - RELAYED

    @pl.when(section == 0)
    def _():
        full(slot_rows, row_send.at[1])
        full(slot_rows, row_send.at[2])
        gone(0, direct - 1, start_send)

    @pl.when(section > 0)
    def _():
        gone(0, direct, start_send)

    for batch in range(SECTIONS):
        gone(1 + batch, direct - 1, second_send.at[batch])

    @pl.when(section < last)
    def _():
        for batch in range(SECTIONS):
            gone(1 + SECTIONS + batch, direct, first_send.at[batch])
        full(landed, land_recv)
        out_ref[...] = landed[...]

    @pl.when(section == last)
    def _():
        full(result.at[pl.ds(0, SECTIONS - 1)], land_send)
        out_ref[...] = result[last]


def per_device(inputs, weights, biases, sources, send_slot):
    slots = send_slot.reshape(2, READERS)
    bf16 = jnp.bfloat16
    pool = (READERS, ROWS, WIDTH)
    grid = (SIDE, SIDE, 2, ROWS, WIDTH)
    rounds = 1 + 2 * SECTIONS
    dma = pltpu.SemaphoreType.DMA
    return pl.pallas_call(
        kernel,
        out_shape=jax.ShapeDtypeStruct((ROWS, BLOCKS * WIDTH), bf16),
        in_specs=[pl.BlockSpec(memory_space=pltpu.HBM)] * 5,
        out_specs=pl.BlockSpec(memory_space=pltpu.VMEM),
        scratch_shapes=[
            pltpu.VMEM((BLOCKS, ROWS, WIDTH), bf16),
            *[pltpu.VMEM(pool, bf16)] * (2 * SECTIONS),
            pltpu.VMEM((SECTIONS, *grid), bf16),
            pltpu.VMEM((SECTIONS, *grid), bf16),
            pltpu.VMEM(grid, bf16),
            pltpu.VMEM(inputs.shape, bf16),
            pltpu.VMEM(weights.shape, bf16),
            pltpu.VMEM(biases.shape, jnp.float32),
            pltpu.SMEM(sources.shape, jnp.int32),
            pltpu.SMEM(slots.shape, jnp.int32),
            pltpu.VMEM(slots.shape, jnp.int32),
            pltpu.VMEM(slots.shape, jnp.int32),
            pltpu.VMEM(slots.shape, jnp.int32),
            pltpu.SMEM(slots.shape, jnp.int32),
            pltpu.SMEM(slots.shape, jnp.int32),
            pltpu.VMEM((SECTIONS, ROWS, BLOCKS * WIDTH), bf16),
            pltpu.VMEM((ROWS, BLOCKS * WIDTH), bf16),
            dma((SECTIONS,)),
            dma((SECTIONS,)),
            dma((SECTIONS,)),
            dma((SECTIONS,)),
            dma(()),
            pltpu.VMEM((rounds, 2, SIDE, ROWS, WIDTH), bf16),
            dma((rounds, 2)),
            dma((rounds,)),
            dma((rounds,)),
            dma((6,)),
            dma((SECTIONS - 1,)),
            dma(()),
            dma(()),
            dma(()),
            dma(()),
            dma(()),
            pltpu.SemaphoreType.REGULAR((2,)),
        ],
        compiler_params=pltpu.CompilerParams(
            collective_id=0, has_side_effects=True, vmem_limit_bytes=60 * 2**20
        ),
        cost_estimate=pl.CostEstimate(flops=2**28, bytes_accessed=2**23, transcendentals=0),
    )(inputs, weights, biases, sources, slots)


def solution(mesh):
    placed = (
        P("segment", "blk"),
        P("segment", "blk", None, None),
        P("segment", "blk"),
        P("segment", "blk", None),
        P("segment", "blk", None, None),
    )
    return jax.shard_map(
        per_device, mesh=mesh, in_specs=placed, out_specs=P("segment", "blk"), check_vma=False
    )
```

time: 151 us -> 160 us (1.060)
  Pallas kernels: 150 us -> 157 us
    pallas_call x1, Pallas kernels: 150 us -> 157 us  [per_device(): pl.pallas_call(kernel, out_shape=jax.ShapeDtypeStruct((ROWS, BLOCKS * WID...]
where the time goes in v1:
time: 160 us; the launch traced here: 158 us
  Pallas kernels  157 us (98%)
    pallas_call x1, Pallas kernels, per_device(): pl.pallas_call(kernel, out_shape=jax.ShapeDtypeStruct((ROWS, BLOCKS * WID...  157 us

profile of v1, /device:TPU:7, one launch (start us, length us, event | category | flops | bytes accessed | tf_op | source)
XLA Modules:
  0.0 158.3 jit_solution(5692490914623258239)
XLA Ops:
  0.0 157.0 %shard_map.55 = bf16[8,512]{1,0:T(8,128)(2,1)} custom-call(bf16[8,512]{1,0:T(8,128)(2,1)} %inputs_hbm.1, bf16[2,4,2048,128]{3,2,1,0:T(8,128)(2,1)} %weights_hbm.1, f32[2,512]{1,0:T(2,128)} %biases_hbm.1, s32[2,4,16]{2,1,0:T(4,128)} %sources_hbm.1, s32[2,128]{1,0:T(2,128)} %bitcast.1), custom_call_target="tpu_custom_call" | custom-call | flops 268435456 | bytes 8388608 | tf_op jit(solution)/shard_map/pallas_call | solution.py:353
  157.0 1.3 copy.7

commit v2 on v1

--- a/solution.py
+++ b/solution.py
@@ -14,8 +14,6 @@
 FAN = 16
 ROWS = 8
 WIDTH = 128
-FAR = (4, 3, 5, 2, 6, 1, 7, 0)
-RELAYED = 2 * SIDE - 1
 
 
 def kernel(
@@ -24,7 +22,6 @@
     first_out, second_out, start_out, inputs_ref, tiles, biases_ref, sources_ref,
     slots_ref, slot_rows, start_rows, next_rows, start_slots, next_slots, result, landed,
     first_recv, second_recv, first_send, second_send, start_send,
-    relay_in, relay_recv, bundle_send, relay_send,
     load_sem, row_send, start_row_recv, next_row_recv, table_sem, land_send, land_recv, hello,
 ):
     first_in = (first_0, first_1, first_2, first_3)
@@ -34,8 +31,6 @@
     z, y, core = me // (2 * SIDE), (me // 2) % SIDE, me % 2
     last = SECTIONS - 1
     middle = SIDE // 2
-    other = 1 - core
-    across_z, across_y = (z + middle) % SIDE, (y + middle) % SIDE
 
     loads = [
         pltpu.make_async_copy(source, target, load_sem.at[i])
@@ -51,27 +46,19 @@
     for load in loads:
         load.start()
 
-    def place(at_z, at_y, at_core):
-        return (at_z * SIDE + at_y) * 2 + at_core
-
     def each_chip(act):
-        def some(step, carry):
-            total = SIDE - step
+        def chip(dz, dy):
+            row = (z + dz + SIDE) % SIDE * SIDE + (y + dy + SIDE) % SIDE
+            act(2 * row)
+            act(2 * row + 1)
+
+        def some(total, carry):
+            total = SIDE - total
 
             def pair(far_z, inner):
                 far_y = total - far_z
                 turn_z = jnp.logical_and(far_z > 0, far_z < middle)
                 turn_y = jnp.logical_and(far_y > 0, far_y < middle)
-                near = jnp.logical_and(far_z < middle, far_y < middle)
-
-                def chip(dz, dy):
-                    at_z, at_y = (z + dz + SIDE) % SIDE, (y + dy + SIDE) % SIDE
-                    act(at_z, at_y, core)
-
-                    @pl.when(near)
-                    def _():
-                        act(at_z, at_y, other)
-
                 chip(far_z, far_y)
 
                 @pl.when(jnp.logical_and(turn_z, turn_y))
@@ -94,22 +81,22 @@
 
     barrier = pltpu.get_barrier_semaphore()
 
-    def greet(step, carry):
-        reader = (me + step) % READERS
+    def greet(reader):
         pl.semaphore_signal(barrier, inc=1, device_id=(section, reader), device_id_type=MESH)
-        return carry
-
+
+    sibling = me + 1 - 2 * core
 
     @pl.when(section == 0)
     def _():
-        for later in range(1, SECTIONS):
-            pl.semaphore_signal(barrier, inc=1, device_id=(later, me), device_id_type=MESH)
+        for other in range(1, SECTIONS):
+            pl.semaphore_signal(barrier, inc=1, device_id=(other, me), device_id_type=MESH)
 
     @pl.when(jnp.logical_and(section > 0, section < last))
     def _():
         pl.semaphore_signal(barrier, inc=1, device_id=(section + 1, me), device_id_type=MESH)
 
-    lax.fori_loop(1, READERS, greet, 0)
+    each_chip(greet)
+    greet(sibling)
     for load in loads[:3]:
         load.wait()
     for block in range(BLOCKS):
@@ -129,66 +116,27 @@
     def full(ref, sem):
         pltpu.make_async_copy(ref, ref, sem).wait()
 
-    def exchange(index, slot_of, outgoing, target, arriving, send_sem, recv_sem, own):
-        def pick(at_z, at_y, at_core):
-            return held[jnp.minimum(slot_of(place(at_z, at_y, at_core)), BLOCKS - 1)]
-
-        def put(at_z, at_y, at_core):
-            outgoing[at_z, at_y, at_core] = pick(at_z, at_y, at_core)
-
-        def post(at_z, at_y, at_core):
-            put(at_z, at_y, at_core)
+    def exchange(slot_of, outgoing, target, arriving, send_sem, recv_sem, own):
+        def put(reader):
+            outgoing[reader] = held[jnp.minimum(slot_of(reader), BLOCKS - 1)]
+
+        def post(reader):
+            put(reader)
             pltpu.make_async_remote_copy(
-                src_ref=outgoing.at[at_z, at_y, at_core],
+                src_ref=outgoing.at[reader],
                 dst_ref=arriving.at[me],
                 send_sem=send_sem,
                 recv_sem=recv_sem,
-                device_id=(target, place(at_z, at_y, at_core)),
+                device_id=(target, reader),
                 device_id_type=MESH,
             ).start()
 
-        for step in range(SIDE):
-            put(step, across_y, other)
-        for step in range(SIDE):
-            put(across_z, step, other)
-        bundles = (
-            (outgoing.at[:, across_y, other], place(z, (y + SIDE - 1) % SIDE, core)),
-            (outgoing.at[across_z, :, other], place((z + SIDE - 1) % SIDE, y, core)),
-        )
-        for side, (bundle, relay_at) in enumerate(bundles):
-            pltpu.make_async_remote_copy(
-                src_ref=bundle,
-                dst_ref=relay_in.at[index, side],
-                send_sem=bundle_send.at[index],
-                recv_sem=relay_recv.at[index, side],
-                device_id=(section, relay_at),
-                device_id_type=MESH,
-            ).start()
         each_chip(post)
-        post(z, y, other)
+        post(sibling)
         if own:
-            arriving[me] = pick(z, y, core)
+            arriving[me] = held[jnp.minimum(slot_of(me), BLOCKS - 1)]
         else:
-            post(z, y, core)
-
-        def forward(side, step, origin, at_z, at_y):
-            pltpu.make_async_remote_copy(
-                src_ref=relay_in.at[index, side, step],
-                dst_ref=arriving.at[origin],
-                send_sem=relay_send.at[index],
-                recv_sem=recv_sem,
-                device_id=(target, place(at_z, at_y, other)),
-                device_id_type=MESH,
-            ).start()
-
-        full(relay_in.at[index, 0], relay_recv.at[index, 0])
-        for far in FAR:
-            step = (z + far) % SIDE
-            forward(0, step, place(z, (y + 1) % SIDE, core), step, (y + 1 + middle) % SIDE)
-        full(relay_in.at[index, 1], relay_recv.at[index, 1])
-        for far in FAR[1:]:
-            step = (y + far) % SIDE
-            forward(1, step, place((z + 1) % SIDE, y, core), (z + 1 + middle) % SIDE, step)
+            post(me)
 
     def arrived(ref, count, sem):
         part = ref.at[pl.ds(0, count)]
@@ -214,7 +162,7 @@
     @pl.when(section == 0)
     def _():
         exchange(
-            0, lambda reader: slots_ref[0, reader],
+            lambda reader: slots_ref[0, reader],
             start_out, 0, first_0, start_send, first_recv.at[0], True,
         )
         full(next_rows, next_row_recv)
@@ -235,7 +183,7 @@
             full(start_rows, start_row_recv)
             to_table(start_rows, start_slots)
             exchange(
-                0, lambda reader: start_slots[0, reader],
+                lambda reader: start_slots[0, reader],
                 start_out, 0, first_in[batch], start_send, first_recv.at[batch], False,
             )
 
@@ -257,7 +205,7 @@
             full(first_in[batch], first_recv.at[batch])
         layer(0, first_in[batch])
         exchange(
-            1 + batch, lambda reader: slots_ref[1, reader], second_out.at[batch], section,
+            lambda reader: slots_ref[1, reader], second_out.at[batch], section,
             second_in[batch], second_send.at[batch], second_recv.at[batch], True,
         )
 
@@ -268,7 +216,7 @@
         @pl.when(section < last)
         def _():
             exchange(
-                1 + SECTIONS + batch, lambda reader: next_slots[0, reader], first_out.at[batch], section + 1,
+                lambda reader: next_slots[0, reader], first_out.at[batch], section + 1,
                 first_in[batch], first_send.at[batch], first_recv.at[batch], False,
             )
 
@@ -310,30 +258,23 @@
 
     full(slot_rows, row_send.at[0])
 
-    def gone(index, count, sem):
-        arrived(first_0, count, sem)
-        full(relay_in.at[index], bundle_send.at[index])
-        arrived(first_0, RELAYED, relay_send.at[index])
-
-    direct = READERS - RELAYED
-
     @pl.when(section == 0)
     def _():
         full(slot_rows, row_send.at[1])
         full(slot_rows, row_send.at[2])
-        gone(0, direct - 1, start_send)
+        arrived(start_out, READERS - 1, start_send)
 
     @pl.when(section > 0)
     def _():
-        gone(0, direct, start_send)
+        full(start_out, start_send)
 
     for batch in range(SECTIONS):
-        gone(1 + batch, direct - 1, second_send.at[batch])
+        arrived(second_out.at[batch], READERS - 1, second_send.at[batch])
 
     @pl.when(section < last)
     def _():
         for batch in range(SECTIONS):
-            gone(1 + SECTIONS + batch, direct, first_send.at[batch])
+            full(first_out.at[batch], first_send.at[batch])
         full(landed, land_recv)
         out_ref[...] = landed[...]
 
@@ -347,8 +288,6 @@
     slots = send_slot.reshape(2, READERS)
     bf16 = jnp.bfloat16
     pool = (READERS, ROWS, WIDTH)
-    grid = (SIDE, SIDE, 2, ROWS, WIDTH)
-    rounds = 1 + 2 * SECTIONS
     dma = pltpu.SemaphoreType.DMA
     return pl.pallas_call(
         kernel,
@@ -358,9 +297,9 @@
         scratch_shapes=[
             pltpu.VMEM((BLOCKS, ROWS, WIDTH), bf16),
             *[pltpu.VMEM(pool, bf16)] * (2 * SECTIONS),
-            pltpu.VMEM((SECTIONS, *grid), bf16),
-            pltpu.VMEM((SECTIONS, *grid), bf16),
-            pltpu.VMEM(grid, bf16),
+            pltpu.VMEM((SECTIONS, *pool), bf16),
+            pltpu.VMEM((SECTIONS, *pool), bf16),
+            pltpu.VMEM(pool, bf16),
             pltpu.VMEM(inputs.shape, bf16),
             pltpu.VMEM(weights.shape, bf16),
             pltpu.VMEM(biases.shape, jnp.float32),
@@ -378,10 +317,6 @@
             dma((SECTIONS,)),
             dma((SECTIONS,)),
             dma(()),
-            pltpu.VMEM((rounds, 2, SIDE, ROWS, WIDTH), bf16),
-            dma((rounds, 2)),
-            dma((rounds,)),
-            dma((rounds,)),
             dma((6,)),
             dma((SECTIONS - 1,)),
             dma(()),

time: 160 us -> 145 us (0.906)
  Pallas kernels: 157 us -> 143 us
    pallas_call x1, Pallas kernels: 157 us -> 143 us  [per_device(): pl.pallas_call(kernel, out_shape=jax.ShapeDtypeStruct((ROWS, BLOCKS * WID...]
where the time goes in v2:
time: 145 us; the launch traced here: 144 us
  Pallas kernels  143 us (99%)
    pallas_call x1, Pallas kernels, per_device(): pl.pallas_call(kernel, out_shape=jax.ShapeDtypeStruct((ROWS, BLOCKS * WID...  143 us

profile of v2, /device:TPU:7, one launch (start us, length us, event | category | flops | bytes accessed | tf_op | source)
XLA Modules:
  0.0 144.4 jit_solution(2058249341005538239)
XLA Ops:
  0.0 143.1 %shard_map.55 = bf16[8,512]{1,0:T(8,128)(2,1)} custom-call(bf16[8,512]{1,0:T(8,128)(2,1)} %inputs_hbm.1, bf16[2,4,2048,128]{3,2,1,0:T(8,128)(2,1)} %weights_hbm.1, f32[2,512]{1,0:T(2,128)} %biases_hbm.1, s32[2,4,16]{2,1,0:T(4,128)} %sources_hbm.1, s32[2,128]{1,0:T(2,128)} %bitcast.1), custom_call_target="tpu_custom_call" | custom-call | flops 268435456 | bytes 8388608 | tf_op jit(solution)/shard_map/pallas_call | solution.py:292
  143.1 1.3 copy.7

commit v3 on v2

--- a/solution.py
+++ b/solution.py
@@ -14,11 +14,13 @@
 FAN = 16
 ROWS = 8
 WIDTH = 128
+PASSED = 2
 
 
 def kernel(
     inputs_hbm, weights_hbm, biases_hbm, sources_hbm, slots_hbm, out_ref,
     held, first_0, first_1, first_2, first_3, second_0, second_1, second_2, second_3,
+    passed_0, passed_1, passed_out, pass_send, pass_recv,
     first_out, second_out, start_out, inputs_ref, tiles, biases_ref, sources_ref,
     slots_ref, slot_rows, start_rows, next_rows, start_slots, next_slots, result, landed,
     first_recv, second_recv, first_send, second_send, start_send,
@@ -26,6 +28,7 @@
 ):
     first_in = (first_0, first_1, first_2, first_3)
     second_in = (second_0, second_1, second_2, second_3)
+    passed_in = (passed_0, passed_1)
     section = lax.axis_index("segment")
     me = lax.axis_index("blk")
     z, y, core = me // (2 * SIDE), (me // 2) % SIDE, me % 2
@@ -116,9 +119,9 @@
     def full(ref, sem):
         pltpu.make_async_copy(ref, ref, sem).wait()
 
-    def exchange(slot_of, outgoing, target, arriving, send_sem, recv_sem, own):
+    def exchange(blocks, slot_of, outgoing, target, arriving, send_sem, recv_sem, own):
         def put(reader):
-            outgoing[reader] = held[jnp.minimum(slot_of(reader), BLOCKS - 1)]
+            outgoing[reader] = blocks[jnp.minimum(slot_of(reader), BLOCKS - 1)]
 
         def post(reader):
             put(reader)
@@ -134,7 +137,7 @@
         each_chip(post)
         post(sibling)
         if own:
-            arriving[me] = held[jnp.minimum(slot_of(me), BLOCKS - 1)]
+            arriving[me] = blocks[jnp.minimum(slot_of(me), BLOCKS - 1)]
         else:
             post(me)
 
@@ -162,7 +165,7 @@
     @pl.when(section == 0)
     def _():
         exchange(
-            lambda reader: slots_ref[0, reader],
+            held, lambda reader: slots_ref[0, reader],
             start_out, 0, first_0, start_send, first_recv.at[0], True,
         )
         full(next_rows, next_row_recv)
@@ -183,7 +186,7 @@
             full(start_rows, start_row_recv)
             to_table(start_rows, start_slots)
             exchange(
-                lambda reader: start_slots[0, reader],
+                held, lambda reader: start_slots[0, reader],
                 start_out, 0, first_in[batch], start_send, first_recv.at[batch], False,
             )
 
@@ -192,20 +195,22 @@
 
     def first(batch):
         if batch == 0:
+            arrived(first_0, READERS - 1, first_recv.at[0])
+        elif batch < PASSED:
 
             @pl.when(section == 0)
             def _():
-                arrived(first_0, READERS - 1, first_recv.at[0])
+                full(first_in[batch], first_recv.at[batch])
 
             @pl.when(section > 0)
             def _():
-                full(first_0, first_recv.at[0])
+                arrived(first_in[batch], READERS - 1, first_recv.at[batch])
 
         else:
             full(first_in[batch], first_recv.at[batch])
         layer(0, first_in[batch])
         exchange(
-            lambda reader: slots_ref[1, reader], second_out.at[batch], section,
+            held, lambda reader: slots_ref[1, reader], second_out.at[batch], section,
             second_in[batch], second_send.at[batch], second_recv.at[batch], True,
         )
 
@@ -215,10 +220,21 @@
 
         @pl.when(section < last)
         def _():
-            exchange(
-                lambda reader: next_slots[0, reader], first_out.at[batch], section + 1,
-                first_in[batch], first_send.at[batch], first_recv.at[batch], False,
-            )
+            if batch < PASSED:
+                passed_out[batch] = held[...]
+                pltpu.make_async_remote_copy(
+                    src_ref=passed_out.at[batch],
+                    dst_ref=passed_in[batch],
+                    send_sem=pass_send.at[batch],
+                    recv_sem=pass_recv.at[batch],
+                    device_id=(section + 1, me),
+                    device_id_type=MESH,
+                ).start()
+            else:
+                exchange(
+                    held, lambda reader: next_slots[0, reader], first_out.at[batch], section + 1,
+                    first_in[batch], first_send.at[batch], first_recv.at[batch], False,
+                )
 
         @pl.when(section == last)
         def _():
@@ -235,6 +251,15 @@
                     device_id_type=MESH,
                 ).start()
 
+    @pl.when(section > 0)
+    def _():
+        for batch in range(PASSED):
+            full(passed_in[batch], pass_recv.at[batch])
+            exchange(
+                passed_in[batch], lambda reader: slots_ref[0, reader], first_out.at[batch], section,
+                first_in[batch], first_send.at[batch], first_recv.at[batch], True,
+            )
+
     first(0)
 
     @pl.when(section == 0)
@@ -250,8 +275,8 @@
 
     first(1)
     second(0)
+    first(2)
     second(1)
-    first(2)
     first(3)
     second(2)
     second(3)
@@ -267,6 +292,8 @@
     @pl.when(section > 0)
     def _():
         full(start_out, start_send)
+        for batch in range(PASSED):
+            arrived(first_out.at[batch], READERS - 1, first_send.at[batch])
 
     for batch in range(SECTIONS):
         arrived(second_out.at[batch], READERS - 1, second_send.at[batch])
@@ -274,7 +301,10 @@
     @pl.when(section < last)
     def _():
         for batch in range(SECTIONS):
-            full(first_out.at[batch], first_send.at[batch])
+            if batch < PASSED:
+                full(passed_out.at[batch], pass_send.at[batch])
+            else:
+                full(first_out.at[batch], first_send.at[batch])
         full(landed, land_recv)
         out_ref[...] = landed[...]
 
@@ -297,6 +327,10 @@
         scratch_shapes=[
             pltpu.VMEM((BLOCKS, ROWS, WIDTH), bf16),
             *[pltpu.VMEM(pool, bf16)] * (2 * SECTIONS),
+            *[pltpu.VMEM((BLOCKS, ROWS, WIDTH), bf16)] * PASSED,
+            pltpu.VMEM((PASSED, BLOCKS, ROWS, WIDTH), bf16),
+            dma((PASSED,)),
+            dma((PASSED,)),
             pltpu.VMEM((SECTIONS, *pool), bf16),
             pltpu.VMEM((SECTIONS, *pool), bf16),
             pltpu.VMEM(pool, bf16),

time: 145 us -> 137 us (0.945)
  Pallas kernels: 143 us -> 136 us
    pallas_call x1, Pallas kernels: 143 us -> 136 us  [per_device(): pl.pallas_call(kernel, out_shape=jax.ShapeDtypeStruct((ROWS, BLOCKS * WID...]
where the time goes in v3:
time: 137 us
  Pallas kernels  136 us (99%)
    pallas_call x1, Pallas kernels, per_device(): pl.pallas_call(kernel, out_shape=jax.ShapeDtypeStruct((ROWS, BLOCKS * WID...  136 us

profile of v3, /device:TPU:7, one launch (start us, length us, event | category | flops | bytes accessed | tf_op | source)
XLA Modules:
  0.0 136.8 jit_solution(4945977969041282165)
XLA Ops:
  0.0 135.5 %shard_map.55 = bf16[8,512]{1,0:T(8,128)(2,1)} custom-call(bf16[8,512]{1,0:T(8,128)(2,1)} %inputs_hbm.1, bf16[2,4,2048,128]{3,2,1,0:T(8,128)(2,1)} %weights_hbm.1, f32[2,512]{1,0:T(2,128)} %biases_hbm.1, s32[2,4,16]{2,1,0:T(4,128)} %sources_hbm.1, s32[2,128]{1,0:T(2,128)} %bitcast.1), custom_call_target="tpu_custom_call" | custom-call | flops 268435456 | bytes 8388608 | tf_op jit(solution)/shard_map/pallas_call | solution.py:322
  135.5 1.3 copy.7

commit v4 on v3

--- a/solution.py
+++ b/solution.py
@@ -14,13 +14,17 @@
 FAN = 16
 ROWS = 8
 WIDTH = 128
-PASSED = 2
+PASSES = ((0, 1, 2), (0, 2))
+PASSED = len(PASSES)
+LENT = ((1, 2), (1, 3), (3, 2))
 
 
 def kernel(
     inputs_hbm, weights_hbm, biases_hbm, sources_hbm, slots_hbm, out_ref,
     held, first_0, first_1, first_2, first_3, second_0, second_1, second_2, second_3,
-    passed_0, passed_1, passed_out, pass_send, pass_recv,
+    passed_0, passed_1, passed_out, pass_send, pass_recv, passed_pool, passed_pool_send,
+    lent_0, lent_1, lent_2, lent_out, lent_pool, lent_send, lent_recv, lent_pool_send,
+    end_rows, end_row_recv, end_slots,
     first_out, second_out, start_out, inputs_ref, tiles, biases_ref, sources_ref,
     slots_ref, slot_rows, start_rows, next_rows, start_slots, next_slots, result, landed,
     first_recv, second_recv, first_send, second_send, start_send,
@@ -29,10 +33,21 @@
     first_in = (first_0, first_1, first_2, first_3)
     second_in = (second_0, second_1, second_2, second_3)
     passed_in = (passed_0, passed_1)
+    lent_in = (lent_0, lent_1, lent_2)
     section = lax.axis_index("segment")
     me = lax.axis_index("blk")
     z, y, core = me // (2 * SIDE), (me // 2) % SIDE, me % 2
     last = SECTIONS - 1
+
+    def is_one_of(sections):
+        found = section < 0
+        for one in sections:
+            found = jnp.logical_or(found, section == one)
+        return found
+
+    def lenders(batch):
+        return [lender for lender, lent in LENT if lent == batch]
+
     middle = SIDE // 2
 
     loads = [
@@ -177,6 +192,10 @@
     def _():
         send_rows(section - 1, next_rows, row_send.at[0], next_row_recv)
 
+    @pl.when(section == last)
+    def _():
+        send_rows(0, end_rows, row_send.at[1], end_row_recv)
+
     for batch in range(1, SECTIONS):
 
         @pl.when(section == batch)
@@ -193,34 +212,55 @@
     for load in loads[3:]:
         load.wait()
 
+    def landed_pool(ref, inside, sem):
+        @pl.when(inside)
+        def _():
+            arrived(ref, READERS - 1, sem)
+
+        @pl.when(jnp.logical_not(inside))
+        def _():
+            full(ref, sem)
+
+    def passes(batch, back):
+        return is_one_of([one + back for one in PASSES[batch]]) if batch < PASSED else section < 0
+
     def first(batch):
+        inside = passes(batch, 1)
         if batch == 0:
-            arrived(first_0, READERS - 1, first_recv.at[0])
-        elif batch < PASSED:
-
-            @pl.when(section == 0)
+            inside = jnp.logical_or(inside, section == 0)
+        landed_pool(first_in[batch], inside, first_recv.at[batch])
+        layer(0, first_in[batch])
+
+        @pl.when(jnp.logical_not(is_one_of(lenders(batch))))
+        def _():
+            exchange(
+                held, lambda reader: slots_ref[1, reader], second_out.at[batch], section,
+                second_in[batch], second_send.at[batch], second_recv.at[batch], True,
+            )
+
+        for i, (lender, lent) in enumerate(LENT):
+            if lent == batch:
+
+                @pl.when(section == lender)
+                def _():
+                    lent_out[i] = held[...]
+                    pltpu.make_async_remote_copy(
+                        src_ref=lent_out.at[i],
+                        dst_ref=lent_in[i],
+                        send_sem=lent_send.at[i],
+                        recv_sem=lent_recv.at[i],
+                        device_id=(0, me),
+                        device_id_type=MESH,
+                    ).start()
+
+    def second(batch):
+        landed_pool(second_in[batch], jnp.logical_not(is_one_of(lenders(batch))), second_recv.at[batch])
+        layer(1, second_in[batch])
+
+        if batch < PASSED:
+
+            @pl.when(passes(batch, 0))
             def _():
-                full(first_in[batch], first_recv.at[batch])
-
-            @pl.when(section > 0)
-            def _():
-                arrived(first_in[batch], READERS - 1, first_recv.at[batch])
-
-        else:
-            full(first_in[batch], first_recv.at[batch])
-        layer(0, first_in[batch])
-        exchange(
-            held, lambda reader: slots_ref[1, reader], second_out.at[batch], section,
-            second_in[batch], second_send.at[batch], second_recv.at[batch], True,
-        )
-
-    def second(batch):
-        arrived(second_in[batch], READERS - 1, second_recv.at[batch])
-        layer(1, second_in[batch])
-
-        @pl.when(section < last)
-        def _():
-            if batch < PASSED:
                 passed_out[batch] = held[...]
                 pltpu.make_async_remote_copy(
                     src_ref=passed_out.at[batch],
@@ -230,11 +270,13 @@
                     device_id=(section + 1, me),
                     device_id_type=MESH,
                 ).start()
-            else:
-                exchange(
-                    held, lambda reader: next_slots[0, reader], first_out.at[batch], section + 1,
-                    first_in[batch], first_send.at[batch], first_recv.at[batch], False,
-                )
+
+        @pl.when(jnp.logical_and(section < last, jnp.logical_not(passes(batch, 0))))
+        def _():
+            exchange(
+                held, lambda reader: next_slots[0, reader], first_out.at[batch], section + 1,
+                first_in[batch], first_send.at[batch], first_recv.at[batch], False,
+            )
 
         @pl.when(section == last)
         def _():
@@ -251,13 +293,14 @@
                     device_id_type=MESH,
                 ).start()
 
-    @pl.when(section > 0)
-    def _():
-        for batch in range(PASSED):
+    for batch in range(PASSED):
+
+        @pl.when(passes(batch, 1))
+        def _():
             full(passed_in[batch], pass_recv.at[batch])
             exchange(
-                passed_in[batch], lambda reader: slots_ref[0, reader], first_out.at[batch], section,
-                first_in[batch], first_send.at[batch], first_recv.at[batch], True,
+                passed_in[batch], lambda reader: slots_ref[0, reader], passed_pool.at[batch], section,
+                first_in[batch], passed_pool_send.at[batch], first_recv.at[batch], True,
             )
 
     first(0)
@@ -281,6 +324,30 @@
     second(2)
     second(3)
 
+    @pl.when(section == 0)
+    def _():
+        full(end_rows, end_row_recv)
+        to_table(end_rows, end_slots)
+        for i, (lender, batch) in enumerate(LENT):
+            table = next_slots if lender == 1 else end_slots
+            full(lent_in[i], lent_recv.at[i])
+            exchange(
+                lent_in[i], lambda reader: table[1, reader], lent_pool.at[i], lender,
+                second_in[batch], lent_pool_send.at[i], second_recv.at[batch], False,
+            )
+        for i in range(len(LENT)):
+            full(lent_pool.at[i], lent_pool_send.at[i])
+
+    for i, (lender, _) in enumerate(LENT):
+
+        @pl.when(section == lender)
+        def _():
+            full(lent_out.at[i], lent_send.at[i])
+
+    @pl.when(section == last)
+    def _():
+        full(slot_rows, row_send.at[1])
+
     full(slot_rows, row_send.at[0])
 
     @pl.when(section == 0)
@@ -292,19 +359,29 @@
     @pl.when(section > 0)
     def _():
         full(start_out, start_send)
-        for batch in range(PASSED):
-            arrived(first_out.at[batch], READERS - 1, first_send.at[batch])
 
     for batch in range(SECTIONS):
-        arrived(second_out.at[batch], READERS - 1, second_send.at[batch])
+
+        @pl.when(jnp.logical_not(is_one_of(lenders(batch))))
+        def _():
+            arrived(second_out.at[batch], READERS - 1, second_send.at[batch])
+
+        if batch < PASSED:
+
+            @pl.when(passes(batch, 0))
+            def _():
+                full(passed_out.at[batch], pass_send.at[batch])
+
+            @pl.when(passes(batch, 1))
+            def _():
+                arrived(passed_pool.at[batch], READERS - 1, passed_pool_send.at[batch])
+
+        @pl.when(jnp.logical_and(section < last, jnp.logical_not(passes(batch, 0))))
+        def _():
+            full(first_out.at[batch], first_send.at[batch])
 
     @pl.when(section < last)
     def _():
-        for batch in range(SECTIONS):
-            if batch < PASSED:
-                full(passed_out.at[batch], pass_send.at[batch])
-            else:
-                full(first_out.at[batch], first_send.at[batch])
         full(landed, land_recv)
         out_ref[...] = landed[...]
 
@@ -331,6 +408,17 @@
             pltpu.VMEM((PASSED, BLOCKS, ROWS, WIDTH), bf16),
             dma((PASSED,)),
             dma((PASSED,)),
+            pltpu.VMEM((PASSED, *pool), bf16),
+            dma((PASSED,)),
+            *[pltpu.VMEM((BLOCKS, ROWS, WIDTH), bf16)] * len(LENT),
+            pltpu.VMEM((len(LENT), BLOCKS, ROWS, WIDTH), bf16),
+            pltpu.VMEM((len(LENT), *pool), bf16),
+            dma((len(LENT),)),
+            dma((len(LENT),)),
+            dma((len(LENT),)),
+            pltpu.VMEM(slots.shape, jnp.int32),
+            dma(()),
+            pltpu.SMEM(slots.shape, jnp.int32),
             pltpu.VMEM((SECTIONS, *pool), bf16),
             pltpu.VMEM((SECTIONS, *pool), bf16),
             pltpu.VMEM(pool, bf16),

time: 137 us -> 140 us (1.022); the launches traced: 137 us -> 138 us
  no operation moved by 1% of the time
where the time goes in v4:
time: 140 us; the launch traced here: 138 us
  Pallas kernels  137 us (98%)
    pallas_call x1, Pallas kernels, per_device(): pl.pallas_call(kernel, out_shape=jax.ShapeDtypeStruct((ROWS, BLOCKS * WID...  137 us

profile of v4, /device:TPU:7, one launch (start us, length us, event | category | flops | bytes accessed | tf_op | source)
XLA Modules:
  0.0 137.9 jit_solution(16949718029353581459)
XLA Ops:
  0.0 136.6 %shard_map.55 = bf16[8,512]{1,0:T(8,128)(2,1)} custom-call(bf16[8,512]{1,0:T(8,128)(2,1)} %inputs_hbm.1, bf16[2,4,2048,128]{3,2,1,0:T(8,128)(2,1)} %weights_hbm.1, f32[2,512]{1,0:T(2,128)} %biases_hbm.1, s32[2,4,16]{2,1,0:T(4,128)} %sources_hbm.1, s32[2,128]{1,0:T(2,128)} %bitcast.1), custom_call_target="tpu_custom_call" | custom-call | flops 268435456 | bytes 8388608 | tf_op jit(solution)/shard_map/pallas_call | solution.py:399
  136.6 1.3 copy.7
